TPU v7x, 32 devices: a whole 2x2x4 slice. The times are simulated.
32 devices in a mesh: dp: 8 (over y, x, core), tp: 4 (over z).
Axes of the slice: x: 2, y: 2, z: 4, core: 2. Of those that a mesh axis runs over, the one named last changes fastest.
Arguments:
- queries: bfloat16 [512, 4, 64, 128], P('dp', None, 'tp'), may hold values from -6 to 6
- new_keys: bfloat16 [512, 4, 8, 128], P('dp', None, 'tp'), may hold values from -6 to 6
- new_values: bfloat16 [512, 4, 8, 128], P('dp', None, 'tp'), may hold values from -6 to 6
- suffix_keys: bfloat16 [512, 256, 8, 128], P('dp', None, 'tp'), may hold values from -6 to 6
- suffix_values: bfloat16 [512, 256, 8, 128], P('dp', None, 'tp'), may hold values from -6 to 6
- suffix_lengths: int32 [512], P('dp'), may hold values from 1 to 256
- prefix_ids: int32 [512, 1], P('dp'), may hold values from 0 to 7; in each aligned block of 64 rows (0 to 63, 64 to 127, ...) at most 16 rows name the same one
- prefix_owner: int32 [8], replicated, may hold values from 0 to 7, each once
- prefix_keys: bfloat16 [8, 2048, 8, 128], P('dp', None, 'tp'), may hold values from -6 to 6
- prefix_values: bfloat16 [8, 2048, 8, 128], P('dp', None, 'tp'), may hold values from -6 to 6
Outputs:
- attended: bfloat16 [512, 4, 64, 128], P('dp', None, 'tp')
Inputs may be any that keep to these rules, and one draw needn't show every extreme that they name: `prefix_ids`: in each aligned block of 64 rows (the rows of one dp index) no prefix is named by more than 16 rows. `prefix_owner`: each dp index stores exactly one prefix.
All inputs are finite; a program needn't handle non-finite values.
Results may differ from a plain program's by a relative error of at most 0.0048.
Values may be sent and summed in bfloat16 or wider, within the bound.
A program may use at most 128 MiB of HBM per device.

v0:
```python
import jax
import jax.numpy as jnp
from jax import lax
from jax.sharding import PartitionSpec as P

NEGATIVE = -1e30


def prefix_partial(grouped, cache_keys, cache_values):
    width = grouped.shape[-1]
    scores = jnp.einsum(
        "nskgd,pkd->nskgp", grouped, cache_keys, preferred_element_type=jnp.float32
    ) * width ** (-0.5)
    highest = jnp.max(scores, axis=-1)
    weights = jnp.exp(scores - highest[..., None])
    total = jnp.sum(weights, axis=-1)
    summed = jnp.einsum(
        "nskgp,pkd->nskgd",
        weights.astype(jnp.bfloat16),
        cache_values,
        preferred_element_type=jnp.float32,
    )
    return (summed, highest, total)


def local_partial(grouped, fresh_keys, fresh_values, cache_keys, cache_values, lengths):
    scale = grouped.shape[-1] ** (-0.5)
    suffix_scores = (
        jnp.einsum("rskgd,rjkd->rskgj", grouped, cache_keys, preferred_element_type=jnp.float32)
        * scale
    )
    fresh_scores = (
        jnp.einsum("rskgd,rtkd->rskgt", grouped, fresh_keys, preferred_element_type=jnp.float32)
        * scale
    )
    positions = jnp.arange(cache_keys.shape[1], dtype=jnp.int32)
    suffix_mask = (positions[None, :] < lengths[:, None])[:, None, None, None, :]
    order = jnp.arange(fresh_keys.shape[1], dtype=jnp.int32)
    fresh_mask = (order[None, :] <= order[:, None])[None, :, None, None, :]
    suffix_scores = jnp.where(suffix_mask, suffix_scores, NEGATIVE)
    fresh_scores = jnp.where(fresh_mask, fresh_scores, NEGATIVE)
    highest = jnp.maximum(jnp.max(suffix_scores, axis=-1), jnp.max(fresh_scores, axis=-1))
    suffix_weights = jnp.where(suffix_mask, jnp.exp(suffix_scores - highest[..., None]), 0.0)
    fresh_weights = jnp.where(fresh_mask, jnp.exp(fresh_scores - highest[..., None]), 0.0)
    total = jnp.sum(suffix_weights, axis=-1) + jnp.sum(fresh_weights, axis=-1)
    summed = jnp.einsum(
        "rskgj,rjkd->rskgd",
        suffix_weights.astype(jnp.bfloat16),
        cache_values,
        preferred_element_type=jnp.float32,
    )
    summed = summed + jnp.einsum(
        "rskgt,rtkd->rskgd",
        fresh_weights.astype(jnp.bfloat16),
        fresh_values,
        preferred_element_type=jnp.float32,
    )
    return (summed, highest, total)


def combine(first, second):
    summed_a, highest_a, total_a = first
    summed_b, highest_b, total_b = second
    highest = jnp.maximum(highest_a, highest_b)
    factor_a = jnp.exp(highest_a - highest)
    factor_b = jnp.exp(highest_b - highest)
    summed = summed_a * factor_a[..., None] + summed_b * factor_b[..., None]
    return (summed, highest, total_a * factor_a + total_b * factor_b)


def on_device(
    queries,
    new_keys,
    new_values,
    suffix_keys,
    suffix_values,
    suffix_lengths,
    prefix_ids,
    prefix_owner,
    prefix_keys,
    prefix_values,
):
    row_count, step_count, head_count, width = queries.shape
    kv_count = new_keys.shape[2]
    grouped = queries.reshape(row_count, step_count, kv_count, head_count // kv_count, width)
    group_count = lax.axis_size("dp")
    capacity = max(2, 2 * row_count // group_count)
    named = prefix_ids == jnp.arange(prefix_owner.shape[0], dtype=jnp.int32)[None, :]
    owner = jnp.sum(jnp.where(named, prefix_owner[None, :], 0), axis=1)
    second = local_partial(
        grouped, new_keys, new_values, suffix_keys, suffix_values, suffix_lengths
    )
    head_shape = grouped.shape[:-1]
    initial = (
        jnp.zeros(grouped.shape, jnp.float32),
        jnp.full(head_shape, NEGATIVE, jnp.float32),
        jnp.zeros(head_shape, jnp.float32),
    )
    slot_rows = jnp.arange(capacity, dtype=jnp.int32)
    carry = initial
    piece_keys = lax.all_gather(prefix_keys, "dp", axis=0, tiled=True)
    piece_values = lax.all_gather(prefix_values, "dp", axis=0, tiled=True)

    def visit(state, item):
        offset, slot_keys, slot_values = item
        chosen = owner == offset
        ranking = jnp.cumsum(chosen.astype(jnp.int32)) - 1
        picking = (chosen[None, :] & (ranking[None, :] == slot_rows[:, None])).astype(jnp.bfloat16)
        picked = jnp.einsum(
            "cr,rskgd->cskgd", picking, grouped, preferred_element_type=jnp.float32
        ).astype(jnp.bfloat16)
        summed, highest, total = prefix_partial(picked, slot_keys, slot_values)
        place = jnp.clip(ranking, 0, capacity - 1)
        keep = chosen[:, None, None, None]
        masked = (
            jnp.where(keep[..., None], jnp.take(summed, place, axis=0), 0.0),
            jnp.where(keep, jnp.take(highest, place, axis=0), NEGATIVE),
            jnp.where(keep, jnp.take(total, place, axis=0), 0.0),
        )
        return (combine(state, masked), None)

    offsets = jnp.arange(piece_keys.shape[0], dtype=jnp.int32)
    carry, unused = lax.scan(visit, carry, (offsets, piece_keys, piece_values))
    summed, highest, total = combine(carry, second)
    return (summed / total[..., None]).reshape(queries.shape).astype(jnp.bfloat16)


def solution(mesh):
    in_specs = (
        P("dp", None, "tp", None),
        P("dp", None, "tp", None),
        P("dp", None, "tp", None),
        P("dp", None, "tp", None),
        P("dp", None, "tp", None),
        P("dp"),
        P("dp", None),
        P(),
        P("dp", None, "tp", None),
        P("dp", None, "tp", None),
    )
    out_specs = P("dp", None, "tp", None)
    return jax.shard_map(
        on_device, mesh=mesh, in_specs=in_specs, out_specs=out_specs, check_vma=False
    )
```

profile of v0, /device:TPU:0, one launch (start us, length us, event | category | flops | bytes accessed | tf_op | source)
XLA Modules:
  0.0 344.2 jit_solution(4898062088969536513)
XLA Ops:
  13.3 4.7 %fusion.72 = (f32[64,4,2,8]{3,1,2,0:T(4,128)S(1)}, f32[64,4,2,8,4]{3,4,1,2,0:T(4,128)S(1)}) fusion(bf16[64,4,2,128,1]{3,2,1,0,4:T(2,128)(2,1)S(1)} %bitcast.121, pred[4,4]{1,0:T(4,128)(4,1)S(1)} %iota_compare_fusion.3, bf16[64,4,16,128]{3,2,1,0:T(8,128)(2,1)S(1)} %copy-done.2), kind=kOutput, calls=%fused_computation.95 | convolution fusion | flops 4239360 | bytes 1261584 | tf_op jit(solution)/shard_map/rskgd,rtkd->rskgt/dot_general | solution.py:33
  18.0 7.5 %bitcast_reduce_fusion.1 = (f32[64,4,2,8]{3,1,2,0:T(4,128)S(1)}, f32[64,2,256,4,8]{2,4,3,1,0:T(8,128)S(1)}) fusion(pred[64,256]{1,0:T(8,128)(4,1)S(1)} %iota_compare_fusion.1, bf16[64,256,2,128,1]{3,2,1,0,4:T(2,128)(2,1)} %bitcast.119, bf16[64,4,16,128]{3,2,1,0:T(8,128)(2,1)S(1)} %copy-done.2), kind=kOutput, calls=%fused_computation.51 | convolution fusion | flops 271577088 | bytes 13664256 | tf_op jit(solution)/shard_map/rskgd,rjkd->rskgj/dot_general | solution.py:29
  30.1 6.2 %fusion.32 = f32[64,2,4,8,128]{4,3,2,1,0:T(8,128)} fusion(bf16[64,256,2,128,1]{3,2,1,0,4:T(2,128)(2,1)} %bitcast.120, f32[64,2,256,4,8]{2,4,3,1,0:T(8,128)S(1)} %get-tuple-element.238, f32[64,4,2,8]{3,1,2,0:T(4,128)S(1)} %max.27, pred[64,256]{1,0:T(8,128)(4,1)S(1)} %iota_compare_fusion.1), kind=kOutput, calls=%fused_computation.46 | convolution fusion | flops 273678336 | bytes 14712832 | tf_op jit(solution)/shard_map/rskgj,rjkd->rskgd/dot_general | solution.py:46
  36.3 30.1 %all-gather.3.cloned.1.call-done = bf16[8,2048,2,128]{3,1,2,0:T(8,128)(2,1)} async-done(((bf16[1,2048,2,128]{3,1,2,0:T(8,128)(2,1)}), bf16[8,2048,2,128]{3,1,2,0:T(8,128)(2,1)}) %all-gather.3.cloned.1.call-update) | async-done | bytes 8388624 | tf_op jit(solution)/shard_map/all_gather | solution.py:101
  66.4 56.3 %all-gather.5.cloned.1.call-done = bf16[8,2048,2,128]{3,1,2,0:T(8,128)(2,1)} async-done(((bf16[1,2048,2,128]{3,1,2,0:T(8,128)(2,1)}), bf16[8,2048,2,128]{3,1,2,0:T(8,128)(2,1)}) %all-gather.5.cloned.1.call-update) | async-done | bytes 8388624 | tf_op jit(solution)/shard_map/all_gather | solution.py:102
  123.2 205.8 %while.17 = (s32[]{:T(128)}, f32[64,4,2,8,128]{4,3,2,1,0:T(8,128)}, f32[64,4,2,8]{0,3,2,1:T(8,128)}, f32[64,4,2,8]{0,3,2,1:T(8,128)}, s32[8]{0:T(128)}, /*index=...) while((s32[]{:T(128)}, f32[64,4,2,8,128]{4,3,2,1,0:T(8,128)}, ...), condition=%wide.region_5.7_spmd.clone, body=%wide.region_1.6_spmd.clone.sunk | while | flops 1110629120 | bytes 74331000 | solution.py:123
  125.4 6.2 %bitcast_reduce_fusion.3 = (f32[16,4,2,8]{0,3,1,2:T(8,128)S(1)}, f32[2,2048,16,4,8]{1,2,4,3,0:T(8,128)}) fusion(bf16[64,4,2,8,128]{4,0,3,1,2:T(8,128)(2,1)} %get-tuple-element.352, s32[64]{0:T(128)S(1)} %get-tuple-element.312, pred[64]{0:T(512)(128)(4,1)S(1)} %get-tuple-element.313, bf16[8,2048,2,128]{3,1,2,0:T(8,128)(2,1)} %get-tuple-element.351, ...), kind=kOutput, calls=%fused_computation.5.clone.1 | convolution fusion | flops 557974528 | bytes 10490180 | tf_op jit(solution)/shard_map/while/body/eval_jaxpr/nskgd,pkd->nskgp/dot_general | solution.py:11
  131.5 4.6 %fusion.91 = f32[16,4,2,8]{0,3,1,2:T(8,128)S(1)} fusion(f32[2,2048,16,4,8]{1,2,4,3,0:T(8,128)} %get-tuple-element.314, f32[16,4,2,8]{0,3,1,2:T(8,128)S(1)} %get-tuple-element.315), kind=kLoop, calls=%fused_computation.7.clone.1 | loop fusion | flops 6290432 | bytes 8396800 | tf_op jit(solution)/shard_map/while/body/eval_jaxpr/reduce_sum | solution.py:16
  143.9 2.8 fusion.93
  148.9 6.2 %bitcast_reduce_fusion.3 = (f32[16,4,2,8]{0,3,1,2:T(8,128)S(1)}, f32[2,2048,16,4,8]{1,2,4,3,0:T(8,128)}) fusion(bf16[64,4,2,8,128]{4,0,3,1,2:T(8,128)(2,1)} %get-tuple-element.352, s32[64]{0:T(128)S(1)} %get-tuple-element.312, pred[64]{0:T(512)(128)(4,1)S(1)} %get-tuple-element.313, bf16[8,2048,2,128]{3,1,2,0:T(8,128)(2,1)} %get-tuple-element.351, ...), kind=kOutput, calls=%fused_computation.5.clone.1 | convolution fusion | flops 557974528 | bytes 10490180 | tf_op jit(solution)/shard_map/while/body/eval_jaxpr/nskgd,pkd->nskgp/dot_general | solution.py:11
  155.1 4.6 %fusion.91 = f32[16,4,2,8]{0,3,1,2:T(8,128)S(1)} fusion(f32[2,2048,16,4,8]{1,2,4,3,0:T(8,128)} %get-tuple-element.314, f32[16,4,2,8]{0,3,1,2:T(8,128)S(1)} %get-tuple-element.315), kind=kLoop, calls=%fused_computation.7.clone.1 | loop fusion | flops 6290432 | bytes 8396800 | tf_op jit(solution)/shard_map/while/body/eval_jaxpr/reduce_sum | solution.py:16
  160.9 2.7 fusion.90
  168.3 4.5 %fusion.93 = f32[64,4,2,8,128]{4,3,2,1,0:T(8,128)} fusion(f32[64,4,2,8,128]{4,3,2,1,0:T(8,128)} %get-tuple-element.335, f32[64,4,2,8,128]{4,3,2,1,0:T(8,128)S(1)} %gather_fusion, f32[64,4,2,8]{3,2,1,0:T(2,128)S(1)} %copy.191, f32[64,4,2,8]{3,2,1,0:T(2,128)S(1)} %copy.192, pred[64]{0:T(512)(128)(4,1)S(1)} %get-tuple-element.318, ...), kind=kLoop, calls=%fused_computation.13.clone.1 | loop fusion | flops 3145728 | bytes 6324353 | tf_op jit(solution)/shard_map/while/body/eval_jaxpr/add | solution.py:67
  175.0 6.2 %bitcast_reduce_fusion.3 = (f32[16,4,2,8]{0,3,1,2:T(8,128)S(1)}, f32[2,2048,16,4,8]{1,2,4,3,0:T(8,128)}) fusion(bf16[64,4,2,8,128]{4,0,3,1,2:T(8,128)(2,1)} %get-tuple-element.352, s32[64]{0:T(128)S(1)} %get-tuple-element.312, pred[64]{0:T(512)(128)(4,1)S(1)} %get-tuple-element.313, bf16[8,2048,2,128]{3,1,2,0:T(8,128)(2,1)} %get-tuple-element.351, ...), kind=kOutput, calls=%fused_computation.5.clone.1 | convolution fusion | flops 557974528 | bytes 10490180 | tf_op jit(solution)/shard_map/while/body/eval_jaxpr/nskgd,pkd->nskgp/dot_general | solution.py:11
  181.1 4.6 %fusion.91 = f32[16,4,2,8]{0,3,1,2:T(8,128)S(1)} fusion(f32[2,2048,16,4,8]{1,2,4,3,0:T(8,128)} %get-tuple-element.314, f32[16,4,2,8]{0,3,1,2:T(8,128)S(1)} %get-tuple-element.315), kind=kLoop, calls=%fused_computation.7.clone.1 | loop fusion | flops 6290432 | bytes 8396800 | tf_op jit(solution)/shard_map/while/body/eval_jaxpr/reduce_sum | solution.py:16
  194.3 4.5 %fusion.93 = f32[64,4,2,8,128]{4,3,2,1,0:T(8,128)} fusion(f32[64,4,2,8,128]{4,3,2,1,0:T(8,128)} %get-tuple-element.335, f32[64,4,2,8,128]{4,3,2,1,0:T(8,128)S(1)} %gather_fusion, f32[64,4,2,8]{3,2,1,0:T(2,128)S(1)} %copy.191, f32[64,4,2,8]{3,2,1,0:T(2,128)S(1)} %copy.192, pred[64]{0:T(512)(128)(4,1)S(1)} %get-tuple-element.318, ...), kind=kLoop, calls=%fused_computation.13.clone.1 | loop fusion | flops 3145728 | bytes 6324353 | tf_op jit(solution)/shard_map/while/body/eval_jaxpr/add | solution.py:67
  201.0 6.2 %bitcast_reduce_fusion.3 = (f32[16,4,2,8]{0,3,1,2:T(8,128)S(1)}, f32[2,2048,16,4,8]{1,2,4,3,0:T(8,128)}) fusion(bf16[64,4,2,8,128]{4,0,3,1,2:T(8,128)(2,1)} %get-tuple-element.352, s32[64]{0:T(128)S(1)} %get-tuple-element.312, pred[64]{0:T(512)(128)(4,1)S(1)} %get-tuple-element.313, bf16[8,2048,2,128]{3,1,2,0:T(8,128)(2,1)} %get-tuple-element.351, ...), kind=kOutput, calls=%fused_computation.5.clone.1 | convolution fusion | flops 557974528 | bytes 10490180 | tf_op jit(solution)/shard_map/while/body/eval_jaxpr/nskgd,pkd->nskgp/dot_general | solution.py:11
  207.2 4.6 %fusion.91 = f32[16,4,2,8]{0,3,1,2:T(8,128)S(1)} fusion(f32[2,2048,16,4,8]{1,2,4,3,0:T(8,128)} %get-tuple-element.314, f32[16,4,2,8]{0,3,1,2:T(8,128)S(1)} %get-tuple-element.315), kind=kLoop, calls=%fused_computation.7.clone.1 | loop fusion | flops 6290432 | bytes 8396800 | tf_op jit(solution)/shard_map/while/body/eval_jaxpr/reduce_sum | solution.py:16
  220.3 4.5 %fusion.93 = f32[64,4,2,8,128]{4,3,2,1,0:T(8,128)} fusion(f32[64,4,2,8,128]{4,3,2,1,0:T(8,128)} %get-tuple-element.335, f32[64,4,2,8,128]{4,3,2,1,0:T(8,128)S(1)} %gather_fusion, f32[64,4,2,8]{3,2,1,0:T(2,128)S(1)} %copy.191, f32[64,4,2,8]{3,2,1,0:T(2,128)S(1)} %copy.192, pred[64]{0:T(512)(128)(4,1)S(1)} %get-tuple-element.318, ...), kind=kLoop, calls=%fused_computation.13.clone.1 | loop fusion | flops 3145728 | bytes 6324353 | tf_op jit(solution)/shard_map/while/body/eval_jaxpr/add | solution.py:67
  227.0 6.2 %bitcast_reduce_fusion.3 = (f32[16,4,2,8]{0,3,1,2:T(8,128)S(1)}, f32[2,2048,16,4,8]{1,2,4,3,0:T(8,128)}) fusion(bf16[64,4,2,8,128]{4,0,3,1,2:T(8,128)(2,1)} %get-tuple-element.352, s32[64]{0:T(128)S(1)} %get-tuple-element.312, pred[64]{0:T(512)(128)(4,1)S(1)} %get-tuple-element.313, bf16[8,2048,2,128]{3,1,2,0:T(8,128)(2,1)} %get-tuple-element.351, ...), kind=kOutput, calls=%fused_computation.5.clone.1 | convolution fusion | flops 557974528 | bytes 10490180 | tf_op jit(solution)/shard_map/while/body/eval_jaxpr/nskgd,pkd->nskgp/dot_general | solution.py:11
  233.2 4.6 %fusion.91 = f32[16,4,2,8]{0,3,1,2:T(8,128)S(1)} fusion(f32[2,2048,16,4,8]{1,2,4,3,0:T(8,128)} %get-tuple-element.314, f32[16,4,2,8]{0,3,1,2:T(8,128)S(1)} %get-tuple-element.315), kind=kLoop, calls=%fused_computation.7.clone.1 | loop fusion | flops 6290432 | bytes 8396800 | tf_op jit(solution)/shard_map/while/body/eval_jaxpr/reduce_sum | solution.py:16
  246.4 4.5 %fusion.93 = f32[64,4,2,8,128]{4,3,2,1,0:T(8,128)} fusion(f32[64,4,2,8,128]{4,3,2,1,0:T(8,128)} %get-tuple-element.335, f32[64,4,2,8,128]{4,3,2,1,0:T(8,128)S(1)} %gather_fusion, f32[64,4,2,8]{3,2,1,0:T(2,128)S(1)} %copy.191, f32[64,4,2,8]{3,2,1,0:T(2,128)S(1)} %copy.192, pred[64]{0:T(512)(128)(4,1)S(1)} %get-tuple-element.318, ...), kind=kLoop, calls=%fused_computation.13.clone.1 | loop fusion | flops 3145728 | bytes 6324353 | tf_op jit(solution)/shard_map/while/body/eval_jaxpr/add | solution.py:67
  253.0 6.2 %bitcast_reduce_fusion.3 = (f32[16,4,2,8]{0,3,1,2:T(8,128)S(1)}, f32[2,2048,16,4,8]{1,2,4,3,0:T(8,128)}) fusion(bf16[64,4,2,8,128]{4,0,3,1,2:T(8,128)(2,1)} %get-tuple-element.352, s32[64]{0:T(128)S(1)} %get-tuple-element.312, pred[64]{0:T(512)(128)(4,1)S(1)} %get-tuple-element.313, bf16[8,2048,2,128]{3,1,2,0:T(8,128)(2,1)} %get-tuple-element.351, ...), kind=kOutput, calls=%fused_computation.5.clone.1 | convolution fusion | flops 557974528 | bytes 10490180 | tf_op jit(solution)/shard_map/while/body/eval_jaxpr/nskgd,pkd->nskgp/dot_general | solution.py:11
  259.2 4.6 %fusion.91 = f32[16,4,2,8]{0,3,1,2:T(8,128)S(1)} fusion(f32[2,2048,16,4,8]{1,2,4,3,0:T(8,128)} %get-tuple-element.314, f32[16,4,2,8]{0,3,1,2:T(8,128)S(1)} %get-tuple-element.315), kind=kLoop, calls=%fused_computation.7.clone.1 | loop fusion | flops 6290432 | bytes 8396800 | tf_op jit(solution)/shard_map/while/body/eval_jaxpr/reduce_sum | solution.py:16
  272.4 4.5 %fusion.93 = f32[64,4,2,8,128]{4,3,2,1,0:T(8,128)} fusion(f32[64,4,2,8,128]{4,3,2,1,0:T(8,128)} %get-tuple-element.335, f32[64,4,2,8,128]{4,3,2,1,0:T(8,128)S(1)} %gather_fusion, f32[64,4,2,8]{3,2,1,0:T(2,128)S(1)} %copy.191, f32[64,4,2,8]{3,2,1,0:T(2,128)S(1)} %copy.192, pred[64]{0:T(512)(128)(4,1)S(1)} %get-tuple-element.318, ...), kind=kLoop, calls=%fused_computation.13.clone.1 | loop fusion | flops 3145728 | bytes 6324353 | tf_op jit(solution)/shard_map/while/body/eval_jaxpr/add | solution.py:67
  279.1 6.2 %bitcast_reduce_fusion.3 = (f32[16,4,2,8]{0,3,1,2:T(8,128)S(1)}, f32[2,2048,16,4,8]{1,2,4,3,0:T(8,128)}) fusion(bf16[64,4,2,8,128]{4,0,3,1,2:T(8,128)(2,1)} %get-tuple-element.352, s32[64]{0:T(128)S(1)} %get-tuple-element.312, pred[64]{0:T(512)(128)(4,1)S(1)} %get-tuple-element.313, bf16[8,2048,2,128]{3,1,2,0:T(8,128)(2,1)} %get-tuple-element.351, ...), kind=kOutput, calls=%fused_computation.5.clone.1 | convolution fusion | flops 557974528 | bytes 10490180 | tf_op jit(solution)/shard_map/while/body/eval_jaxpr/nskgd,pkd->nskgp/dot_general | solution.py:11
  285.2 4.6 %fusion.91 = f32[16,4,2,8]{0,3,1,2:T(8,128)S(1)} fusion(f32[2,2048,16,4,8]{1,2,4,3,0:T(8,128)} %get-tuple-element.314, f32[16,4,2,8]{0,3,1,2:T(8,128)S(1)} %get-tuple-element.315), kind=kLoop, calls=%fused_computation.7.clone.1 | loop fusion | flops 6290432 | bytes 8396800 | tf_op jit(solution)/shard_map/while/body/eval_jaxpr/reduce_sum | solution.py:16
  298.4 4.5 %fusion.93 = f32[64,4,2,8,128]{4,3,2,1,0:T(8,128)} fusion(f32[64,4,2,8,128]{4,3,2,1,0:T(8,128)} %get-tuple-element.335, f32[64,4,2,8,128]{4,3,2,1,0:T(8,128)S(1)} %gather_fusion, f32[64,4,2,8]{3,2,1,0:T(2,128)S(1)} %copy.191, f32[64,4,2,8]{3,2,1,0:T(2,128)S(1)} %copy.192, pred[64]{0:T(512)(128)(4,1)S(1)} %get-tuple-element.318, ...), kind=kLoop, calls=%fused_computation.13.clone.1 | loop fusion | flops 3145728 | bytes 6324353 | tf_op jit(solution)/shard_map/while/body/eval_jaxpr/add | solution.py:67
  305.1 6.2 %bitcast_reduce_fusion.3 = (f32[16,4,2,8]{0,3,1,2:T(8,128)S(1)}, f32[2,2048,16,4,8]{1,2,4,3,0:T(8,128)}) fusion(bf16[64,4,2,8,128]{4,0,3,1,2:T(8,128)(2,1)} %get-tuple-element.352, s32[64]{0:T(128)S(1)} %get-tuple-element.312, pred[64]{0:T(512)(128)(4,1)S(1)} %get-tuple-element.313, bf16[8,2048,2,128]{3,1,2,0:T(8,128)(2,1)} %get-tuple-element.351, ...), kind=kOutput, calls=%fused_computation.5.clone.1 | convolution fusion | flops 557974528 | bytes 10490180 | tf_op jit(solution)/shard_map/while/body/eval_jaxpr/nskgd,pkd->nskgp/dot_general | solution.py:11
  311.3 4.6 %fusion.91 = f32[16,4,2,8]{0,3,1,2:T(8,128)S(1)} fusion(f32[2,2048,16,4,8]{1,2,4,3,0:T(8,128)} %get-tuple-element.314, f32[16,4,2,8]{0,3,1,2:T(8,128)S(1)} %get-tuple-element.315), kind=kLoop, calls=%fused_computation.7.clone.1 | loop fusion | flops 6290432 | bytes 8396800 | tf_op jit(solution)/shard_map/while/body/eval_jaxpr/reduce_sum | solution.py:16
  324.4 4.5 %fusion.93 = f32[64,4,2,8,128]{4,3,2,1,0:T(8,128)} fusion(f32[64,4,2,8,128]{4,3,2,1,0:T(8,128)} %get-tuple-element.335, f32[64,4,2,8,128]{4,3,2,1,0:T(8,128)S(1)} %gather_fusion, f32[64,4,2,8]{3,2,1,0:T(2,128)S(1)} %copy.191, f32[64,4,2,8]{3,2,1,0:T(2,128)S(1)} %copy.192, pred[64]{0:T(512)(128)(4,1)S(1)} %get-tuple-element.318, ...), kind=kLoop, calls=%fused_computation.13.clone.1 | loop fusion | flops 3145728 | bytes 6324353 | tf_op jit(solution)/shard_map/while/body/eval_jaxpr/add | solution.py:67
  332.0 4.2 %fusion.43 = bf16[64,4,2,8,128]{4,3,1,2,0:T(8,128)(2,1)S(1)} fusion(f32[64,4,2,8,128]{4,3,2,1,0:T(8,128)} %get-tuple-element.133, f32[64,2,4,8,128]{4,3,2,1,0:T(8,128)} %fusion.32, f32[64,4,2,8]{3,1,2,0:T(4,128)S(1)} %bitcast.116, f32[64,4,2,8]{3,1,2,0:T(4,128)S(1)} %bitcast.118, f32[64,4,2,8]{3,1,2,0:T(4,128)S(1)} %bitcast.117, ...), kind=kOutput, calls=%fused_computation.60 | convolution fusion | flops 7389184 | bytes 5505040 | tf_op jit(solution)/shard_map/rskgt,rtkd->rskgd/dot_general | solution.py:52
  (212 shorter events, 97.6 us)
Async XLA Ops:
  6.5 325.4 %copy-start = (bf16[64,4,2,128]{3,2,1,0:T(2,128)(2,1)S(1)}, bf16[64,4,2,128]{3,2,1,0:T(2,128)(2,1)}, u32[]{:S(2)}) copy-start(bf16[64,4,2,128]{3,2,1,0:T(2,128)(2,1)} %param.16) | copy-start | bytes 393220
  6.5 5.0 %copy-start.2 = (bf16[64,4,16,128]{3,2,1,0:T(8,128)(2,1)S(1)}, bf16[64,4,16,128]{3,2,1,0:T(8,128)(2,1)}, u32[]{:S(2)}) copy-start(bf16[64,4,16,128]{3,2,1,0:T(8,128)(2,1)} %param.14) | copy-start | bytes 3145732
  6.5 6.6 %copy-start.5 = (s32[64]{0:T(128)S(1)}, s32[64]{0:T(128)}, u32[]{:S(2)}) copy-start(s32[64]{0:T(128)} %param.19) | copy-start | bytes 772
  6.5 6.7 %copy-start.6 = (bf16[64,4,2,128]{3,2,1,0:T(2,128)(2,1)S(1)}, bf16[64,4,2,128]{3,2,1,0:T(2,128)(2,1)}, u32[]{:S(2)}) copy-start(bf16[64,4,2,128]{3,2,1,0:T(2,128)(2,1)} %param.15) | copy-start | bytes 393220
  6.5 59.8 %all-gather.3.cloned.1.call-start = ((), (), s32[]{:S(2)}) async-start(), calls=%async_computation | async-start | bytes 9437184 | tf_op jit(solution)/shard_map/all_gather | solution.py:101
  9.0 113.7 %all-gather.5.cloned.1.call-start = ((), (), s32[]{:S(2)}) async-start(), calls=%async_computation.1 | async-start | bytes 9437184 | tf_op jit(solution)/shard_map/all_gather | solution.py:102
  13.2 12.5 %copy-start.4 = (pred[4,4]{1,0:T(4,128)(4,1)}, pred[4,4]{1,0:T(4,128)(4,1)S(1)}, u32[]{:S(2)}) copy-start(pred[4,4]{1,0:T(4,128)(4,1)S(1)} %iota_compare_fusion.3) | copy-start | bytes 52
  18.0 18.3 %copy-start.3 = (f32[64,4,2,8,4]{3,4,1,2,0:T(4,128)}, f32[64,4,2,8,4]{3,4,1,2,0:T(4,128)S(1)}, u32[]{:S(2)}) copy-start(f32[64,4,2,8,4]{3,4,1,2,0:T(4,128)S(1)} %get-tuple-element.240) | copy-start | bytes 196612
  18.0 7.6 %copy-start.7 = (s32[8]{0:T(128)S(1)}, s32[8]{0:T(128)}, u32[]{:S(2)}) copy-start(s32[8]{0:T(128)} %param.21) | copy-start | bytes 100
  18.0 7.6 %copy-start.8 = (s32[64,1]{0,1:T(1,128)S(1)}, s32[64,1]{0,1:T(1,128)}, u32[]{:S(2)}) copy-start(s32[64,1]{0,1:T(1,128)} %param.20) | copy-start | bytes 772
  131.5 5.8 %copy-start.1 = (f32[2,2048,16,4,8]{1,2,4,3,0:T(8,128)S(1)}, f32[2,2048,16,4,8]{1,2,4,3,0:T(8,128)}, u32[]{:S(2)}) copy-start(f32[2,2048,16,4,8]{1,2,4,3,0:T(8,128)} %get-tuple-element.314) | copy-start | bytes 25165828 | tf_op jit(solution)/shard_map/while
  155.1 5.8 %copy-start.1 = (f32[2,2048,16,4,8]{1,2,4,3,0:T(8,128)S(1)}, f32[2,2048,16,4,8]{1,2,4,3,0:T(8,128)}, u32[]{:S(2)}) copy-start(f32[2,2048,16,4,8]{1,2,4,3,0:T(8,128)} %get-tuple-element.314) | copy-start | bytes 25165828 | tf_op jit(solution)/shard_map/while
  181.1 5.8 %copy-start.1 = (f32[2,2048,16,4,8]{1,2,4,3,0:T(8,128)S(1)}, f32[2,2048,16,4,8]{1,2,4,3,0:T(8,128)}, u32[]{:S(2)}) copy-start(f32[2,2048,16,4,8]{1,2,4,3,0:T(8,128)} %get-tuple-element.314) | copy-start | bytes 25165828 | tf_op jit(solution)/shard_map/while
  207.2 5.8 %copy-start.1 = (f32[2,2048,16,4,8]{1,2,4,3,0:T(8,128)S(1)}, f32[2,2048,16,4,8]{1,2,4,3,0:T(8,128)}, u32[]{:S(2)}) copy-start(f32[2,2048,16,4,8]{1,2,4,3,0:T(8,128)} %get-tuple-element.314) | copy-start | bytes 25165828 | tf_op jit(solution)/shard_map/while
  233.2 5.8 %copy-start.1 = (f32[2,2048,16,4,8]{1,2,4,3,0:T(8,128)S(1)}, f32[2,2048,16,4,8]{1,2,4,3,0:T(8,128)}, u32[]{:S(2)}) copy-start(f32[2,2048,16,4,8]{1,2,4,3,0:T(8,128)} %get-tuple-element.314) | copy-start | bytes 25165828 | tf_op jit(solution)/shard_map/while
  259.2 5.8 %copy-start.1 = (f32[2,2048,16,4,8]{1,2,4,3,0:T(8,128)S(1)}, f32[2,2048,16,4,8]{1,2,4,3,0:T(8,128)}, u32[]{:S(2)}) copy-start(f32[2,2048,16,4,8]{1,2,4,3,0:T(8,128)} %get-tuple-element.314) | copy-start | bytes 25165828 | tf_op jit(solution)/shard_map/while
  285.2 5.8 %copy-start.1 = (f32[2,2048,16,4,8]{1,2,4,3,0:T(8,128)S(1)}, f32[2,2048,16,4,8]{1,2,4,3,0:T(8,128)}, u32[]{:S(2)}) copy-start(f32[2,2048,16,4,8]{1,2,4,3,0:T(8,128)} %get-tuple-element.314) | copy-start | bytes 25165828 | tf_op jit(solution)/shard_map/while
  311.3 5.8 %copy-start.1 = (f32[2,2048,16,4,8]{1,2,4,3,0:T(8,128)S(1)}, f32[2,2048,16,4,8]{1,2,4,3,0:T(8,128)}, u32[]{:S(2)}) copy-start(f32[2,2048,16,4,8]{1,2,4,3,0:T(8,128)} %get-tuple-element.314) | copy-start | bytes 25165828 | tf_op jit(solution)/shard_map/while
Sparse Core Ops, SparseCore 0:
  9.3 57.0 all-gather.2
  68.3 54.3 all-gather.4
where the time goes:
time: 346 us; the launch traced here: 344 us
  other arithmetic  93.9 us (27%)
  matrix products  93.7 us (27%)
  waiting for transfers between devices  86.5 us (25%)
  local copies, waits for them, and re-layouts  55.8 us (16%)
  between operations  13.6 us (4%)
    all_gather x1, waiting for transfers between devices, on_device(): piece_values = lax.all_gather(prefix_values, 'dp', axis=0, tiled=True)  56.3 us
    dot_general x8, matrix products, prefix_partial(): jnp.einsum('nskgd,pkd->nskgp', grouped, cache_keys, preferred_element_typ...  49.4 us
    reduce_sum x8, other arithmetic, prefix_partial(): total = jnp.sum(weights, axis=-1)  36.7 us
    add x8, other arithmetic, combine(): summed = summed_a * factor_a[..., None] + summed_b * factor_b[..., None]  34.6 us
    all_gather x1, waiting for transfers between devices, on_device(): piece_keys = lax.all_gather(prefix_keys, 'dp', axis=0, tiled=True)  30.1 us
    dot_general x8, matrix products, prefix_partial(): jnp.einsum('nskgp,pkd->nskgd', weights.astype(jnp.bfloat16), cache_values...  21.7 us
    add x9, other arithmetic, combine(): return (summed, highest, total_a * factor_a + total_b * factor_b)  11.7 us
    while x16, local copies, waits for them, and re-layouts  10 us
  transfers between devices with their start and end apart: 2, of which 2 were waited for; matrix products, arithmetic and copies ran while one was open for 8% of the time, Pallas kernels for 0%

commit v1 on v0

v1 whole, which is shorter than its diff:
```python
import functools
import math

import jax
import jax.numpy as jnp
from jax import lax
from jax.experimental import pallas as pl
from jax.experimental.pallas import tpu as pltpu
from jax.sharding import PartitionSpec as P

NEGATIVE = -1e30
LOG2E = math.log2(math.e)
MESH = pl.DeviceIdType.MESH
F32 = jnp.float32
BF16 = jnp.bfloat16


def place_kernel(cap, ids_ref, owner_ref, pick_ref, slot_ref, count_ref):
    def clear(i, _):
        pick_ref[i] = 0
        return 0

    lax.fori_loop(0, pick_ref.shape[0], clear, 0)

    def clear_count(i, _):
        count_ref[i] = 0
        return 0

    lax.fori_loop(0, count_ref.shape[0], clear_count, 0)

    def place(r, _):
        owner = owner_ref[ids_ref[r]]
        rank = count_ref[owner]
        count_ref[owner] = rank + 1
        slot = owner * cap + rank
        slot_ref[r] = slot
        pick_ref[slot] = r
        return 0

    lax.fori_loop(0, ids_ref.shape[0], place, 0)


def dot_t(a, b):
    return lax.dot_general(a, b, (((1,), (1,)), ((), ())), preferred_element_type=F32)


def dot(a, b):
    return lax.dot_general(a, b, (((1,), (0,)), ((), ())), preferred_element_type=F32)


def swap_groups(x, outer, inner):
    return jnp.concatenate(
        [x[(o * inner + i) * 8 : (o * inner + i) * 8 + 8] for i in range(inner) for o in range(outer)],
        axis=0,
    )


def kernel(
    n,
    cap,
    kvs,
    steps,
    chunks,
    pick_ref,
    slot_ref,
    len_ref,
    q_hbm,
    nk_ref,
    nv_ref,
    sk_hbm,
    sv_hbm,
    pk_hbm,
    pv_hbm,
    out_ref,
    q_raw,
    q_perm,
    q_send,
    q_recv,
    r_send,
    r_recv,
    t_send,
    t_recv,
    p_raw,
    wide,
    keys,
    values,
    sk,
    sv,
    own_a,
    own_l,
    q_sem,
    p_sem,
    s_sem,
    qs_sem,
    qr_sem,
    rs_sem,
    rr_sem,
    ts_sem,
    tr_sem,
):
    rows, heads, width = q_raw.shape
    per = heads // kvs
    plen = keys.shape[1]
    slots = sk.shape[1]
    scale = width ** (-0.5) * LOG2E
    me = lax.axis_index("dp")

    load_q = pltpu.make_async_copy(q_hbm, q_raw, q_sem)
    load_q.start()
    load_k = pltpu.make_async_copy(pk_hbm, p_raw.at[0], p_sem.at[0])
    load_v = pltpu.make_async_copy(pv_hbm, p_raw.at[1], p_sem.at[1])
    load_k.start()
    load_v.start()
    step = rows // chunks

    def suffix_copies(c):
        part = pl.ds(c * step, step)
        return (
            pltpu.make_async_copy(sk_hbm.at[part], sk.at[part], s_sem.at[0, c]),
            pltpu.make_async_copy(sv_hbm.at[part], sv.at[part], s_sem.at[1, c]),
        )

    barrier = pltpu.get_barrier_semaphore()

    def greet(k, _):
        pl.semaphore_signal(barrier, inc=1, device_id={"dp": lax.rem(me + k, n)}, device_id_type=MESH)
        return 0

    lax.fori_loop(1, n, greet, 0)

    load_q.wait()

    def permute(r, _):
        x = q_raw[r].astype(F32)
        q_perm[r] = swap_groups(x, steps, kvs).astype(BF16)
        return 0

    lax.fori_loop(0, rows, permute, 0)

    def choose(peer, ref):
        def one(j, _):
            s = peer * cap + j
            ref[peer, j] = q_perm[pick_ref[s]]
            return 0

        lax.fori_loop(0, cap, one, 0)

    def q_copy(peer, source):
        return pltpu.make_async_remote_copy(
            src_ref=q_send.at[peer],
            dst_ref=q_recv.at[source],
            send_sem=qs_sem.at[peer],
            recv_sem=qr_sem.at[source],
            device_id={"dp": peer},
            device_id_type=MESH,
        )

    def r_copy(peer, source):
        return pltpu.make_async_remote_copy(
            src_ref=r_send.at[peer],
            dst_ref=r_recv.at[source],
            send_sem=rs_sem.at[peer],
            recv_sem=rr_sem.at[source],
            device_id={"dp": peer},
            device_id_type=MESH,
        )

    def t_copy(peer, source):
        return pltpu.make_async_remote_copy(
            src_ref=t_send.at[peer],
            dst_ref=t_recv.at[source],
            send_sem=ts_sem.at[peer],
            recv_sem=tr_sem.at[source],
            device_id={"dp": peer},
            device_id_type=MESH,
        )

    pl.semaphore_wait(barrier, n - 1)

    def send(k, _):
        peer = lax.rem(me + k, n)
        choose(peer, q_send)
        q_copy(peer, me).start()
        return 0

    lax.fori_loop(1, n, send, 0)
    choose(me, q_recv)

    def start_suffix(c, _):
        for copy in suffix_copies(c):
            copy.start()
        return 0

    lax.fori_loop(0, chunks, start_suffix, 0)

    load_k.wait()
    load_v.wait()
    piece = wide.shape[0] // kvs

    def split(c, _):
        for which in range(2):
            wide[...] = p_raw[which, pl.ds(c * piece * kvs, piece * kvs), :].astype(F32)
            for kv in range(kvs):
                part = wide[pl.ds(kv, piece, stride=kvs), :].astype(BF16)
                if which == 0:
                    keys[kv, pl.ds(c * piece, piece), :] = part
                else:
                    values[kv, pl.ds(c * piece, piece), 0:width] = part
                    values[kv, pl.ds(c * piece, piece), width : 2 * width] = jnp.ones((piece, width), BF16)
        return 0

    lax.fori_loop(0, plen // piece, split, 0)

    group = min(cap, 8)
    lane = lax.broadcasted_iota(jnp.int32, (per, width), 1)
    line = lax.broadcasted_iota(jnp.int32, (per, width), 0)

    def attend(source):
        def part(c, _):
            where = pl.ds(c * group, group)
            stat = jnp.zeros((group, width), F32)
            for kv in range(kvs):
                q = q_recv[source, where, kv * per : (kv + 1) * per, :].reshape(group * per, width)
                s = dot_t(q, keys[kv])
                top = jnp.max(s, axis=-1, keepdims=True) * scale
                w = jnp.exp2(s * scale - top).astype(BF16)
                both = dot(w, values[kv])
                total = both[:, width : 2 * width]
                a = both[:, 0:width] / total
                r_send[source, where, kv * per : (kv + 1) * per, :] = a.astype(BF16).reshape(group, per, width)
                level = (top + jnp.log(total) * LOG2E).reshape(group, per, width)
                stat = stat + jnp.sum(jnp.where((lane == line + kv * per)[None], level, 0.0), axis=1)
            t_send[source, where, :, :] = stat.reshape(group, 1, width)
            return 0

        lax.fori_loop(0, cap // group, part, 0)

    attend(me)

    fresh = nk_ref.shape[0] // rows
    row = lax.broadcasted_iota(jnp.int32, (heads, slots), 0)
    col = lax.broadcasted_iota(jnp.int32, (heads, slots), 1)
    same = lax.rem(col, kvs) == row // per
    position = jnp.where(same, col // kvs, slots)
    nrow = lax.broadcasted_iota(jnp.int32, (2 * heads, 2 * fresh), 0)
    ncol = lax.broadcasted_iota(jnp.int32, (2 * heads, 2 * fresh), 1)
    nrow_in, ncol_in = lax.rem(nrow, heads), lax.rem(ncol, fresh)
    fresh_mask = (
        (nrow // heads == ncol // fresh)
        & (nrow_in // per == lax.rem(ncol_in, kvs))
        & (ncol_in // kvs <= lax.rem(nrow_in, per) // (per // steps))
    )

    def local(pair):
        first = pair * 2
        q2 = q_perm[pl.ds(first, 2)].reshape(2 * heads, width)
        new = pl.ds(pl.multiple_of(pair * 2 * fresh, 2 * fresh), 2 * fresh)
        sn = jnp.where(fresh_mask, dot_t(q2, nk_ref[new, :]), NEGATIVE)
        top_n = jnp.max(sn, axis=-1, keepdims=True)
        scores, tops = [], []
        for i in range(2):
            s = dot_t(q2[i * heads : (i + 1) * heads], sk[first + i])
            s = jnp.where(position < len_ref[first + i], s, NEGATIVE)
            scores.append(s)
            tops.append(jnp.maximum(jnp.max(s, axis=-1, keepdims=True), top_n[i * heads : (i + 1) * heads]))
        top = jnp.concatenate(tops, axis=0)
        wn = jnp.exp2((sn - top) * scale)
        total_n = jnp.sum(wn, axis=-1, keepdims=True)
        un = dot(wn.astype(BF16), nv_ref[new, :])
        for i in range(2):
            half = slice(i * heads, (i + 1) * heads)
            w = jnp.exp2((scores[i] - tops[i]) * scale)
            total = jnp.sum(w, axis=-1, keepdims=True) + total_n[half]
            u = dot(w.astype(BF16), sv[first + i]) + un[half]
            own_a[first + i] = u / total
            own_l[first + i] = tops[i] * scale + jnp.log(total) * LOG2E

    def local_chunk(c, _):
        for copy in suffix_copies(c):
            copy.wait()

        def one(i, _):
            local(c * (step // 2) + i)
            return 0

        lax.fori_loop(0, step // 2, one, 0)
        return 0

    lax.fori_loop(0, chunks, local_chunk, 0)

    def serve(k, _):
        source = lax.rem(me + n - k, n)
        q_copy(source, source).wait_recv()
        attend(source)
        r_copy(source, me).start()
        t_copy(source, me).start()
        return 0

    lax.fori_loop(1, n, serve, 0)

    r_recv[me] = r_send[me]
    t_recv[me] = t_send[me]

    def finish(k, _):
        peer = lax.rem(me + k, n)
        r_copy(peer, peer).wait_recv()
        t_copy(peer, peer).wait_recv()
        return 0

    lax.fori_loop(1, n, finish, 0)

    lane_h = lax.broadcasted_iota(jnp.int32, (heads, width), 1)
    line_h = lax.broadcasted_iota(jnp.int32, (heads, width), 0)

    def merge(r, _):
        place = slot_ref[r]
        a1 = r_recv[place // cap, lax.rem(place, cap)].astype(F32)
        stat = t_recv[place // cap, lax.rem(place, cap)]
        level = jnp.sum(jnp.where(lane_h == line_h, stat, 0.0), axis=1, keepdims=True)
        share = 1.0 / (1.0 + jnp.exp2(own_l[r] - level))
        a2 = own_a[r]
        out = a2 + (a1 - a2) * share
        out_ref[r] = swap_groups(out, kvs, steps).astype(BF16)
        return 0

    lax.fori_loop(0, rows, merge, 0)

    def drain(k, _):
        peer = lax.rem(me + k, n)
        q_copy(peer, me).wait_send()
        r_copy(peer, me).wait_send()
        t_copy(peer, me).wait_send()
        return 0

    lax.fori_loop(1, n, drain, 0)


def on_device(
    n,
    queries,
    new_keys,
    new_values,
    suffix_keys,
    suffix_values,
    suffix_lengths,
    prefix_ids,
    prefix_owner,
    prefix_keys,
    prefix_values,
):
    rows, steps, head_count, width = queries.shape
    kvs = new_keys.shape[2]
    heads = steps * head_count
    slen = suffix_keys.shape[1]
    plen = prefix_keys.shape[1]
    cap = max(2, 2 * rows // n)
    chunks = 8
    smem = pl.BlockSpec(memory_space=pltpu.SMEM)
    vmem = pl.BlockSpec(memory_space=pltpu.VMEM)
    hbm = pl.BlockSpec(memory_space=pl.ANY)

    pick, slot = pl.pallas_call(
        functools.partial(place_kernel, cap),
        out_shape=(
            jax.ShapeDtypeStruct((n * cap,), jnp.int32),
            jax.ShapeDtypeStruct((rows,), jnp.int32),
        ),
        in_specs=[smem, smem],
        out_specs=(smem, smem),
        scratch_shapes=[pltpu.SMEM((n,), jnp.int32)],
    )(prefix_ids.reshape(rows), prefix_owner)

    flops = 4 * n * cap * heads * plen * width + 4 * rows * heads * kvs * slen * width
    out = pl.pallas_call(
        functools.partial(kernel, n, cap, kvs, steps, chunks),
        out_shape=jax.ShapeDtypeStruct((rows, heads, width), BF16),
        in_specs=[smem, smem, smem, hbm, vmem, vmem, hbm, hbm, hbm, hbm],
        out_specs=vmem,
        scratch_shapes=[
            pltpu.VMEM((rows, heads, width), BF16),
            pltpu.VMEM((rows, heads, width), BF16),
            pltpu.VMEM((n, cap, heads, width), BF16),
            pltpu.VMEM((n, cap, heads, width), BF16),
            pltpu.VMEM((n, cap, heads, width), BF16),
            pltpu.VMEM((n, cap, heads, width), BF16),
            pltpu.VMEM((n, cap, 1, width), F32),
            pltpu.VMEM((n, cap, 1, width), F32),
            pltpu.VMEM((2, plen * kvs, width), BF16),
            pltpu.VMEM((256 * kvs, width), F32),
            pltpu.VMEM((kvs, plen, width), BF16),
            pltpu.VMEM((kvs, plen, 2 * width), BF16),
            pltpu.VMEM((rows, slen * kvs, width), BF16),
            pltpu.VMEM((rows, slen * kvs, width), BF16),
            pltpu.VMEM((rows, heads, width), F32),
            pltpu.VMEM((rows, heads, 1), F32),
            pltpu.SemaphoreType.DMA,
            pltpu.SemaphoreType.DMA((2,)),
            pltpu.SemaphoreType.DMA((2, chunks)),
            pltpu.SemaphoreType.DMA((n,)),
            pltpu.SemaphoreType.DMA((n,)),
            pltpu.SemaphoreType.DMA((n,)),
            pltpu.SemaphoreType.DMA((n,)),
            pltpu.SemaphoreType.DMA((n,)),
            pltpu.SemaphoreType.DMA((n,)),
        ],
        compiler_params=pltpu.CompilerParams(
            collective_id=0, has_side_effects=True, vmem_limit_bytes=58 * 1024 * 1024
        ),
        cost_estimate=pl.CostEstimate(
            flops=flops, bytes_accessed=24 * 1024 * 1024, transcendentals=n * cap * heads * plen
        ),
    )(
        pick,
        slot,
        suffix_lengths,
        queries.reshape(rows, heads, width),
        new_keys.reshape(rows * steps * kvs, width),
        new_values.reshape(rows * steps * kvs, width),
        suffix_keys.reshape(rows, slen * kvs, width),
        suffix_values.reshape(rows, slen * kvs, width),
        prefix_keys.reshape(plen * kvs, width),
        prefix_values.reshape(plen * kvs, width),
    )
    return out.reshape(queries.shape)


def solution(mesh):
    in_specs = (
        P("dp", None, "tp", None),
        P("dp", None, "tp", None),
        P("dp", None, "tp", None),
        P("dp", None, "tp", None),
        P("dp", None, "tp", None),
        P("dp"),
        P("dp", None),
        P(),
        P("dp", None, "tp", None),
        P("dp", None, "tp", None),
    )
    out_specs = P("dp", None, "tp", None)
    return jax.shard_map(
        functools.partial(on_device, mesh.shape["dp"]),
        mesh=mesh,
        in_specs=in_specs,
        out_specs=out_specs,
        check_vma=False,
    )
```

time: 346 us -> 86.9 us (0.25)
  other arithmetic: 93.9 us -> 0 us
  matrix products: 93.7 us -> 0 us
  waiting for transfers between devices: 86.5 us -> 0 us
  Pallas kernels: 0 us -> 84.3 us
  local copies, waits for them, and re-layouts: 55.8 us -> 2.38 us
  between operations: 13.6 us -> 0.02 us
    dot_general x20 -> x0, matrix products: 93.7 us -> none  [the longest x8 49.4 us: prefix_partial(): jnp.einsum('nskgd,pkd->nskgp', grouped, cache_keys, preferred_element_typ...]
    all_gather x2 -> x0, waiting for transfers between devices: 86.4 us -> none  [the longest x1 56.3 us: on_device(): piece_values = lax.all_gather(prefix_values, 'dp', axis=0, tiled=True)]
    pallas_call x0 -> x2, Pallas kernels: none -> 84.3 us  [the longest x1 81.2 us: on_device(): pl.pallas_call(functools.partial(kernel, n, cap, kvs, steps, chunks), out...]
    add x17 -> x0, other arithmetic: 46.2 us -> none  [the longest x8 34.6 us: combine(): summed = summed_a * factor_a[..., None] + summed_b * factor_b[..., None]]
    reduce_sum x11 -> x0, other arithmetic: 41.1 us -> none  [the longest x8 36.7 us: prefix_partial(): total = jnp.sum(weights, axis=-1)]
    gather x40 -> x0, local copies, waits for them, and re-layouts: 19 us -> none  [the longest x16 6.81 us: visit(): jnp.take(highest, place, axis=0)]
    while x18 -> x0, local copies, waits for them, and re-layouts: 11.8 us -> none
    dynamic_slice x8 -> x0, local copies, waits for them, and re-layouts: 9.86 us -> none  [on_device(): carry, unused = lax.scan(visit, carry, (offsets, piece_keys, piece_values))]
  transfers between devices with their start and end apart: 2 -> 0, of which waited for: 2 -> 0; matrix products, arithmetic and copies ran while one was open for 8% -> 0% of each run, Pallas kernels for 0% -> 0%
where the time goes in v1:
time: 86.9 us; the launch traced here: 86.7 us
  Pallas kernels  84.3 us (97%)
  local copies, waits for them, and re-layouts  2.38 us (3%)
    pallas_call x1, Pallas kernels, on_device(): pl.pallas_call(functools.partial(kernel, n, cap, kvs, steps, chunks), out...  81.2 us
    pallas_call x1, Pallas kernels, on_device(): pl.pallas_call(functools.partial(place_kernel, cap), out_shape=(jax.Shape...  3.13 us
    unnamed x1, local copies, waits for them, and re-layouts  2.38 us

profile of v1, /device:TPU:0, one launch (start us, length us, event | category | flops | bytes accessed | tf_op | source)
XLA Modules:
  0.0 86.7 jit_solution(17680948102035379269)
XLA Ops:
  0.0 3.1 %shard_map.100 = (s32[128]{0:T(128)}, s32[64]{0:T(128)}) custom-call(s32[64]{0:T(128)} %bitcast.17, s32[8]{0:T(128)} %owner_ref.1), custom_call_target="tpu_custom_call" | custom-call | tf_op jit(solution)/shard_map/pallas_call | solution.py:362
  3.1 81.2 %shard_map.101 = bf16[64,64,128]{2,1,0:T(8,128)(2,1)} custom-call(s32[128]{0:T(128)} %get-tuple-element.7.pick_ref, s32[64]{0:T(128)} %get-tuple-element.8.slot_ref, s32[64]{0:T(128)} %len_ref.1, bf16[64,64,128]{2,1,0:T(8,128)(2,1)} %bitcast.12, bf16[512,128]{1,0:T(8,128)(2,1)} %bitcast.15, bf16[512,128]{1,0:T(8,128)(2,1)} %bitcast.16, ...), custom_call_target="tpu_custom_call" | custom-call | flops 9663676416 | bytes 25165824 | tf_op jit(solution)/shard_map/pallas_call | solution.py:374
  84.3 2.4 %copy.12 = bf16[64,4,16,128]{3,2,1,0:T(8,128)(2,1)} copy(bf16[64,4,16,128]{3,2,1,0:T(8,128)(2,1)} %bitcast.9) | data formatting | bytes 2097152

commit v2 on v1

v2 whole, which is shorter than its diff:
```python
import functools
import math

import jax
import jax.numpy as jnp
from jax import lax
from jax.experimental import pallas as pl
from jax.experimental.pallas import tpu as pltpu
from jax.sharding import PartitionSpec as P

NEGATIVE = -1e30
LOG2E = math.log2(math.e)
MESH = pl.DeviceIdType.MESH
F32 = jnp.float32
BF16 = jnp.bfloat16


def place(ids, owner_ref, cap, table):
    rows, lanes = ids.shape[1], table.shape[1]
    owner = jnp.zeros((1, rows), jnp.int32)
    for p in range(owner_ref.shape[0]):
        owner = owner + jnp.where(ids == p, owner_ref[p], 0)
    down = lax.broadcasted_iota(jnp.int32, (rows, rows), 0)
    across = lax.broadcasted_iota(jnp.int32, (rows, rows), 1)

    def column(row):
        return jnp.sum(jnp.where(down == across, row, 0), axis=1, keepdims=True)

    earlier = (column(owner) == owner) & (down < across)
    slot = owner * cap + jnp.sum(jnp.where(earlier, 1, 0), axis=0, keepdims=True)
    here = column(slot) == lax.broadcasted_iota(jnp.int32, (rows, lanes), 1)
    request = lax.broadcasted_iota(jnp.int32, (rows, lanes), 0)
    table[...] = jnp.zeros_like(table)
    table[0:1, 0:rows] = slot
    table[1:2, :] = jnp.sum(jnp.where(here, request, 0), axis=0, keepdims=True)


def dot_t(a, b):
    return lax.dot_general(a, b, (((1,), (1,)), ((), ())), preferred_element_type=F32)


def dot(a, b):
    return lax.dot_general(a, b, (((1,), (0,)), ((), ())), preferred_element_type=F32)


def partner(me, k, n):
    if n & (n - 1):
        return lax.rem(me + k, n)
    total, bit = 0, 1
    while bit < n:
        mine, other = lax.rem(me // bit, 2), lax.rem(k // bit, 2)
        total = total + bit * (mine + other - 2 * mine * other)
        bit *= 2
    return total


def source_of(me, k, n):
    return lax.rem(me + n - k, n) if n & (n - 1) else partner(me, k, n)


def turn(i, n):
    if n % 2:
        return i
    half = n // 2 - 1
    return jnp.where(i == 1, 1, (lax.rem(i - 2, half) + 1) * 2 + (i - 2) // half)


def kernel(
    n,
    cap,
    kvs,
    steps,
    fresh,
    chunks,
    ids_ref,
    owner_ref,
    len_ref,
    q_hbm,
    nk_hbm,
    nv_hbm,
    sk_hbm,
    sv_hbm,
    pk_hbm,
    pv_hbm,
    out_hbm,
    table,
    places,
    nk_ref,
    nv_ref,
    out_ref,
    level_ref,
    q_raw,
    q_send,
    q_recv,
    r_send,
    r_recv,
    t_send,
    t_recv,
    p_raw,
    wide,
    keys,
    values,
    sk,
    sv,
    own_a,
    own_l,
    table_sem,
    n_sem,
    o_sem,
    q_sem,
    p_sem,
    s_sem,
    qs_sem,
    qr_sem,
    rs_sem,
    rr_sem,
    ts_sem,
    tr_sem,
):
    rows, heads, width = q_raw.shape
    per = heads // kvs
    plen = keys.shape[1]
    slots = sk.shape[1]
    scale = width ** (-0.5) * LOG2E
    me = lax.axis_index("dp")

    load_q = pltpu.make_async_copy(q_hbm, q_raw, q_sem)
    load_q.start()
    load_k = pltpu.make_async_copy(pk_hbm, p_raw.at[0], p_sem.at[0])
    load_v = pltpu.make_async_copy(pv_hbm, p_raw.at[1], p_sem.at[1])
    load_k.start()
    load_v.start()
    load_nk = pltpu.make_async_copy(nk_hbm, nk_ref, n_sem.at[0])
    load_nv = pltpu.make_async_copy(nv_hbm, nv_ref, n_sem.at[1])
    load_nk.start()
    load_nv.start()
    step = rows // chunks

    def suffix_copies(c):
        part = pl.ds(c * step, step)
        return (
            pltpu.make_async_copy(sk_hbm.at[part], sk.at[part], s_sem.at[0, c]),
            pltpu.make_async_copy(sv_hbm.at[part], sv.at[part], s_sem.at[1, c]),
        )

    barrier = pltpu.get_barrier_semaphore()

    def greet(k, _):
        pl.semaphore_signal(barrier, inc=1, device_id={"dp": lax.rem(me + k, n)}, device_id_type=MESH)
        return 0

    lax.fori_loop(1, n, greet, 0)

    place(ids_ref[...], owner_ref, cap, table)
    put = pltpu.make_async_copy(table, places, table_sem)
    put.start()
    put.wait()
    load_q.wait()

    def choose(peer, ref):
        def one(j, _):
            s = peer * cap + j
            ref[peer, j] = q_raw[places[1, s]]
            return 0

        lax.fori_loop(0, cap, one, 0)

    def q_copy(peer, source):
        return pltpu.make_async_remote_copy(
            src_ref=q_send.at[peer],
            dst_ref=q_recv.at[source],
            send_sem=qs_sem.at[peer],
            recv_sem=qr_sem.at[source],
            device_id={"dp": peer},
            device_id_type=MESH,
        )

    def r_copy(peer, source):
        return pltpu.make_async_remote_copy(
            src_ref=r_send.at[peer],
            dst_ref=r_recv.at[source],
            send_sem=rs_sem.at[peer],
            recv_sem=rr_sem.at[source],
            device_id={"dp": peer},
            device_id_type=MESH,
        )

    def t_copy(peer, source):
        return pltpu.make_async_remote_copy(
            src_ref=t_send.at[peer],
            dst_ref=t_recv.at[source],
            send_sem=ts_sem.at[peer],
            recv_sem=tr_sem.at[source],
            device_id={"dp": peer},
            device_id_type=MESH,
        )

    pl.semaphore_wait(barrier, n - 1)

    def send(i, _):
        peer = partner(me, turn(i, n), n)
        choose(peer, q_send)
        q_copy(peer, me).start()
        return 0

    lax.fori_loop(1, n, send, 0)
    choose(me, q_recv)

    def start_suffix(c, _):
        for copy in suffix_copies(c):
            copy.start()
        return 0

    lax.fori_loop(0, chunks, start_suffix, 0)

    load_k.wait()
    load_v.wait()
    piece = wide.shape[0] // kvs

    def split(c, _):
        for which in range(2):
            wide[...] = p_raw[which, pl.ds(c * piece * kvs, piece * kvs), :].astype(F32)
            for kv in range(kvs):
                part = wide[pl.ds(kv, piece, stride=kvs), :].astype(BF16)
                if which == 0:
                    keys[kv, pl.ds(c * piece, piece), :] = part
                else:
                    values[kv, pl.ds(c * piece, piece), 0:width] = part
                    values[kv, pl.ds(c * piece, piece), width : 2 * width] = jnp.ones((piece, width), BF16)
        return 0

    lax.fori_loop(0, plen // piece, split, 0)

    gq = per // steps
    lane = lax.broadcasted_iota(jnp.int32, (per, width), 1)
    line = lax.broadcasted_iota(jnp.int32, (per, width), 0)
    natural = (line // gq) * (gq * kvs) + lax.rem(line, gq)

    def attend(source):
        grouped = q_recv[source].astype(F32).reshape(cap * steps, kvs, gq, width)
        scores = [
            dot_t(grouped[:, kv].reshape(cap * per, width).astype(BF16), keys[kv]) for kv in range(kvs)
        ]
        stat = jnp.zeros((cap, width), F32)
        parts = []
        for kv in range(kvs):
            s = scores[kv]
            top = jnp.max(s, axis=-1, keepdims=True) * scale
            w = jnp.exp2(s * scale - top).astype(BF16)
            both = dot(w, values[kv])
            total = both[:, width : 2 * width]
            parts.append((both[:, 0:width] / total).reshape(cap * steps, 1, gq, width))
            level = (top + jnp.log(total) * LOG2E).reshape(cap, per, width)
            stat = stat + jnp.sum(jnp.where((lane == natural + kv * gq)[None], level, 0.0), axis=1)
        joined = jnp.concatenate(parts, axis=1) if kvs > 1 else parts[0]
        r_send[source] = joined.reshape(cap, heads, width).astype(BF16)
        t_send[source] = stat.reshape(cap, 1, width)

    early = chunks // 2

    attend(me)

    row = lax.broadcasted_iota(jnp.int32, (heads, slots), 0)
    col = lax.broadcasted_iota(jnp.int32, (heads, slots), 1)
    same = lax.rem(col, kvs) == lax.rem(row // gq, kvs)
    position = jnp.where(same, col // kvs, slots)
    many = 4
    nrow = lax.broadcasted_iota(jnp.int32, (many * heads, many * fresh), 0)
    ncol = lax.broadcasted_iota(jnp.int32, (many * heads, many * fresh), 1)
    nrow_in, ncol_in = lax.rem(nrow, heads), lax.rem(ncol, fresh)
    fresh_mask = (
        (nrow // heads == ncol // fresh)
        & (lax.rem(nrow_in // gq, kvs) == lax.rem(ncol_in, kvs))
        & (ncol_in // kvs <= nrow_in // (gq * kvs))
    )

    def local(index):
        first = index * many
        q = q_raw[pl.ds(first, many)].reshape(many * heads, width)
        new = pl.ds(pl.multiple_of(index * many * fresh, many * fresh), many * fresh)
        half = [slice(i * heads, (i + 1) * heads) for i in range(many)]
        scores = [dot_t(q[half[i]], sk[first + i]) for i in range(many)]
        sn = jnp.where(fresh_mask, dot_t(q, nk_ref[new, :]), NEGATIVE)
        top_n = jnp.max(sn, axis=-1, keepdims=True)
        scores = [jnp.where(position < len_ref[first + i], scores[i], NEGATIVE) for i in range(many)]
        tops = [
            jnp.maximum(jnp.max(scores[i], axis=-1, keepdims=True), top_n[half[i]]) for i in range(many)
        ]
        wn = jnp.exp2((sn - jnp.concatenate(tops, axis=0)) * scale)
        total_n = jnp.sum(wn, axis=-1, keepdims=True)
        un = dot(wn.astype(BF16), nv_ref[new, :])
        weights = [jnp.exp2((scores[i] - tops[i]) * scale) for i in range(many)]
        summed = [dot(weights[i].astype(BF16), sv[first + i]) for i in range(many)]
        for i in range(many):
            total = jnp.sum(weights[i], axis=-1, keepdims=True) + total_n[half[i]]
            own_a[first + i] = (summed[i] + un[half[i]]) / total
            own_l[first + i] = jnp.broadcast_to(tops[i] * scale + jnp.log(total) * LOG2E, (heads, width))

    load_nk.wait()
    load_nv.wait()

    def local_chunk(c, _):
        for copy in suffix_copies(c):
            copy.wait()

        def one(i, _):
            local(c * (step // many) + i)
            return 0

        lax.fori_loop(0, step // many, one, 0)
        return 0

    lax.fori_loop(0, early, local_chunk, 0)

    def serve(i, _):
        source = source_of(me, turn(i, n), n)
        q_copy(source, source).wait_recv()
        attend(source)
        r_copy(source, me).start()
        t_copy(source, me).start()
        return 0

    lax.fori_loop(1, n, serve, 0)
    lax.fori_loop(early, chunks, local_chunk, 0)

    r_recv[me] = r_send[me]
    t_recv[me] = t_send[me]

    spread = lax.broadcasted_iota(jnp.int32, (cap, heads, width), 2) == lax.broadcasted_iota(
        jnp.int32, (cap, heads, width), 1
    )

    def widen(owner):
        level = jnp.sum(jnp.where(spread, t_recv[owner], 0.0), axis=2, keepdims=True)
        level_ref[owner] = jnp.broadcast_to(level, (cap, heads, width))

    widen(me)

    def finish(i, _):
        peer = partner(me, turn(i, n), n)
        t_copy(peer, peer).wait_recv()
        widen(peer)
        r_copy(peer, peer).wait_recv()
        return 0

    lax.fori_loop(1, n, finish, 0)

    def out_copy(c):
        part = pl.ds(c * step, step)
        return pltpu.make_async_copy(out_ref.at[part], out_hbm.at[part], o_sem.at[c])

    def merge_chunk(c, _):
        def merge(index, _):
            first = c * step + index * many
            results = []
            for i in range(many):
                slot = places[0, first + i]
                owner, rank = slot // cap, lax.rem(slot, cap)
                a1 = r_recv[owner, rank].astype(F32)
                share = 1.0 / (1.0 + jnp.exp2(own_l[first + i] - level_ref[owner, rank]))
                a2 = own_a[first + i]
                results.append((a2 + (a1 - a2) * share).astype(BF16))
            for i in range(many):
                out_ref[first + i] = results[i]
            return 0

        lax.fori_loop(0, step // many, merge, 0)
        out_copy(c).start()
        return 0

    lax.fori_loop(0, chunks, merge_chunk, 0)

    def drain_out(c, _):
        out_copy(c).wait()
        return 0

    lax.fori_loop(0, chunks, drain_out, 0)

    def drain(k, _):
        peer = lax.rem(me + k, n)
        q_copy(peer, me).wait_send()
        r_copy(peer, me).wait_send()
        t_copy(peer, me).wait_send()
        return 0

    lax.fori_loop(1, n, drain, 0)


def on_device(
    n,
    queries,
    new_keys,
    new_values,
    suffix_keys,
    suffix_values,
    suffix_lengths,
    prefix_ids,
    prefix_owner,
    prefix_keys,
    prefix_values,
):
    rows, steps, head_count, width = queries.shape
    kvs = new_keys.shape[2]
    heads = steps * head_count
    slen = suffix_keys.shape[1]
    plen = prefix_keys.shape[1]
    cap = max(2, 2 * rows // n)
    chunks = 4
    smem = pl.BlockSpec(memory_space=pltpu.SMEM)
    vmem = pl.BlockSpec(memory_space=pltpu.VMEM)
    hbm = pl.BlockSpec(memory_space=pl.ANY)

    flops = 4 * n * cap * heads * plen * width + 4 * rows * heads * kvs * slen * width
    out = pl.pallas_call(
        functools.partial(kernel, n, cap, kvs, steps, steps * kvs, chunks),
        out_shape=jax.ShapeDtypeStruct((rows, heads, width), BF16),
        in_specs=[vmem, smem, smem, hbm, hbm, hbm, hbm, hbm, hbm, hbm],
        out_specs=hbm,
        scratch_shapes=[
            pltpu.VMEM((2, n * cap), jnp.int32),
            pltpu.SMEM((2, n * cap), jnp.int32),
            pltpu.VMEM((rows * steps * kvs, width), BF16),
            pltpu.VMEM((rows * steps * kvs, width), BF16),
            pltpu.VMEM((rows, heads, width), BF16),
            pltpu.VMEM((n, cap, heads, width), F32),
            pltpu.VMEM((rows, heads, width), BF16),
            pltpu.VMEM((n, cap, heads, width), BF16),
            pltpu.VMEM((n, cap, heads, width), BF16),
            pltpu.VMEM((n, cap, heads, width), BF16),
            pltpu.VMEM((n, cap, heads, width), BF16),
            pltpu.VMEM((n, cap, 1, width), F32),
            pltpu.VMEM((n, cap, 1, width), F32),
            pltpu.VMEM((2, plen * kvs, width), BF16),
            pltpu.VMEM((256 * kvs, width), F32),
            pltpu.VMEM((kvs, plen, width), BF16),
            pltpu.VMEM((kvs, plen, 2 * width), BF16),
            pltpu.VMEM((rows, slen * kvs, width), BF16),
            pltpu.VMEM((rows, slen * kvs, width), BF16),
            pltpu.VMEM((rows, heads, width), F32),
            pltpu.VMEM((rows, heads, width), F32),
            pltpu.SemaphoreType.DMA,
            pltpu.SemaphoreType.DMA((2,)),
            pltpu.SemaphoreType.DMA((chunks,)),
            pltpu.SemaphoreType.DMA,
            pltpu.SemaphoreType.DMA((2,)),
            pltpu.SemaphoreType.DMA((2, chunks)),
            pltpu.SemaphoreType.DMA((n,)),
            pltpu.SemaphoreType.DMA((n,)),
            pltpu.SemaphoreType.DMA((n,)),
            pltpu.SemaphoreType.DMA((n,)),
            pltpu.SemaphoreType.DMA((n,)),
            pltpu.SemaphoreType.DMA((n,)),
        ],
        compiler_params=pltpu.CompilerParams(
            collective_id=0, has_side_effects=True, vmem_limit_bytes=58 * 1024 * 1024
        ),
        cost_estimate=pl.CostEstimate(
            flops=flops, bytes_accessed=24 * 1024 * 1024, transcendentals=n * cap * heads * plen
        ),
    )(
        prefix_ids.reshape(1, rows),
        prefix_owner,
        suffix_lengths,
        queries.reshape(rows, heads, width),
        new_keys.reshape(rows * steps * kvs, width),
        new_values.reshape(rows * steps * kvs, width),
        suffix_keys.reshape(rows, slen * kvs, width),
        suffix_values.reshape(rows, slen * kvs, width),
        prefix_keys.reshape(plen * kvs, width),
        prefix_values.reshape(plen * kvs, width),
    )
    return out.reshape(queries.shape)


def solution(mesh):
    in_specs = (
        P("dp", None, "tp", None),
        P("dp", None, "tp", None),
        P("dp", None, "tp", None),
        P("dp", None, "tp", None),
        P("dp", None, "tp", None),
        P("dp"),
        P("dp", None),
        P(),
        P("dp", None, "tp", None),
        P("dp", None, "tp", None),
    )
    out_specs = P("dp", None, "tp", None)
    return jax.shard_map(
        functools.partial(on_device, mesh.shape["dp"]),
        mesh=mesh,
        in_specs=in_specs,
        out_specs=out_specs,
        check_vma=False,
    )
```

time: 86.9 us -> 57.6 us (0.66)
  Pallas kernels: 84.3 us -> 54.8 us
    pallas_call x2 -> x1, Pallas kernels: 84.3 us -> 54.8 us  [on_device(): pl.pallas_call(functools.partial(kernel, n, cap, kvs, steps, steps * kvs,...]
where the time goes in v2:
time: 57.6 us; the launch traced here: 57.2 us
  Pallas kernels  54.8 us (95%)
  local copies, waits for them, and re-layouts  2.38 us (4%)
    pallas_call x1, Pallas kernels, on_device(): pl.pallas_call(functools.partial(kernel, n, cap, kvs, steps, steps * kvs,...  54.8 us
    unnamed x1, local copies, waits for them, and re-layouts  2.38 us

profile of v2, /device:TPU:0, one launch (start us, length us, event | category | flops | bytes accessed | tf_op | source)
XLA Modules:
  0.0 57.2 jit_solution(12423181535658581728)
XLA Ops:
  0.0 54.8 %shard_map.100 = bf16[64,64,128]{2,1,0:T(8,128)(2,1)} custom-call(s32[1,64]{1,0:T(1,128)} %bitcast.17, s32[8]{0:T(128)} %owner_ref.1, s32[64]{0:T(128)} %len_ref.1, bf16[64,64,128]{2,1,0:T(8,128)(2,1)} %bitcast.12, bf16[512,128]{1,0:T(8,128)(2,1)} %bitcast.15, bf16[512,128]{1,0:T(8,128)(2,1)} %bitcast.16, bf16[64,512,128]{2,1,0:T(8,128)(2,1)} %bitcast.10, ...), custom_call_target="tpu_custom_call" | custom-call | flops 9663676416 | bytes 25165824 | tf_op jit(solution)/shard_map/pallas_call | solution.py:414
  54.8 2.4 %copy.12 = bf16[64,4,16,128]{3,2,1,0:T(8,128)(2,1)} copy(bf16[64,4,16,128]{3,2,1,0:T(8,128)(2,1)} %bitcast.9) | data formatting | bytes 2097152

commit v3 on v2

--- a/solution.py
+++ b/solution.py
@@ -62,7 +62,7 @@
     if n % 2:
         return i
     half = n // 2 - 1
-    return jnp.where(i == 1, 1, (lax.rem(i - 2, half) + 1) * 2 + (i - 2) // half)
+    return jnp.where(i == 1, 1, (half - lax.rem(i - 2, half)) * 2 + (i - 2) // half)
 
 
 def kernel(
@@ -235,6 +235,8 @@
     lane = lax.broadcasted_iota(jnp.int32, (per, width), 1)
     line = lax.broadcasted_iota(jnp.int32, (per, width), 0)
     natural = (line // gq) * (gq * kvs) + lax.rem(line, gq)
+    fold = cap // t_send.shape[1]
+    offset = lax.rem(lax.broadcasted_iota(jnp.int32, (cap, per, width), 0), fold) * heads
 
     def attend(source):
         grouped = q_recv[source].astype(F32).reshape(cap * steps, kvs, gq, width)
@@ -251,10 +253,10 @@
             total = both[:, width : 2 * width]
             parts.append((both[:, 0:width] / total).reshape(cap * steps, 1, gq, width))
             level = (top + jnp.log(total) * LOG2E).reshape(cap, per, width)
-            stat = stat + jnp.sum(jnp.where((lane == natural + kv * gq)[None], level, 0.0), axis=1)
+            stat = stat + jnp.sum(jnp.where(offset == (lane - natural - kv * gq)[None], level, 0.0), axis=1)
         joined = jnp.concatenate(parts, axis=1) if kvs > 1 else parts[0]
         r_send[source] = joined.reshape(cap, heads, width).astype(BF16)
-        t_send[source] = stat.reshape(cap, 1, width)
+        t_send[source] = jnp.sum(stat.reshape(cap // fold, fold, width), axis=1, keepdims=True)
 
     early = chunks // 2
 
@@ -316,8 +318,8 @@
         source = source_of(me, turn(i, n), n)
         q_copy(source, source).wait_recv()
         attend(source)
+        t_copy(source, me).start()
         r_copy(source, me).start()
-        t_copy(source, me).start()
         return 0
 
     lax.fori_loop(1, n, serve, 0)
@@ -326,13 +328,17 @@
     r_recv[me] = r_send[me]
     t_recv[me] = t_send[me]
 
-    spread = lax.broadcasted_iota(jnp.int32, (cap, heads, width), 2) == lax.broadcasted_iota(
-        jnp.int32, (cap, heads, width), 1
-    )
+    shared = (cap // fold, heads, width)
+    spread = lax.broadcasted_iota(jnp.int32, shared, 2) - lax.broadcasted_iota(jnp.int32, shared, 1)
 
     def widen(owner):
-        level = jnp.sum(jnp.where(spread, t_recv[owner], 0.0), axis=2, keepdims=True)
-        level_ref[owner] = jnp.broadcast_to(level, (cap, heads, width))
+        stat = t_recv[owner]
+        levels = []
+        for f in range(fold):
+            level = jnp.sum(jnp.where(spread == f * heads, stat, 0.0), axis=2, keepdims=True)
+            levels.append(jnp.broadcast_to(level, shared).reshape(cap // fold, 1, heads, width))
+        joined = jnp.concatenate(levels, axis=1) if fold > 1 else levels[0]
+        level_ref[owner] = joined.reshape(cap, heads, width)
 
     widen(me)
 
@@ -406,6 +412,7 @@
     plen = prefix_keys.shape[1]
     cap = max(2, 2 * rows // n)
     chunks = 4
+    fold = math.gcd(cap, max(1, width // heads))
     smem = pl.BlockSpec(memory_space=pltpu.SMEM)
     vmem = pl.BlockSpec(memory_space=pltpu.VMEM)
     hbm = pl.BlockSpec(memory_space=pl.ANY)
@@ -428,8 +435,8 @@
             pltpu.VMEM((n, cap, heads, width), BF16),
             pltpu.VMEM((n, cap, heads, width), BF16),
             pltpu.VMEM((n, cap, heads, width), BF16),
-            pltpu.VMEM((n, cap, 1, width), F32),
-            pltpu.VMEM((n, cap, 1, width), F32),
+            pltpu.VMEM((n, cap // fold, 1, width), F32),
+            pltpu.VMEM((n, cap // fold, 1, width), F32),
             pltpu.VMEM((2, plen * kvs, width), BF16),
             pltpu.VMEM((256 * kvs, width), F32),
             pltpu.VMEM((kvs, plen, width), BF16),

time: 57.6 us -> 56.8 us (0.986)
  no operation moved by 1% of the time
where the time goes in v3:
time: 56.8 us; the launch traced here: 56.7 us
  Pallas kernels  54.3 us (96%)
  local copies, waits for them, and re-layouts  2.38 us (4%)
    pallas_call x1, Pallas kernels, on_device(): pl.pallas_call(functools.partial(kernel, n, cap, kvs, steps, steps * kvs,...  54.3 us
    unnamed x1, local copies, waits for them, and re-layouts  2.38 us

profile of v3, /device:TPU:0, one launch (start us, length us, event | category | flops | bytes accessed | tf_op | source)
XLA Modules:
  0.0 56.7 jit_solution(2199447931922385779)
XLA Ops:
  0.0 54.3 %shard_map.100 = bf16[64,64,128]{2,1,0:T(8,128)(2,1)} custom-call(s32[1,64]{1,0:T(1,128)} %bitcast.17, s32[8]{0:T(128)} %owner_ref.1, s32[64]{0:T(128)} %len_ref.1, bf16[64,64,128]{2,1,0:T(8,128)(2,1)} %bitcast.12, bf16[512,128]{1,0:T(8,128)(2,1)} %bitcast.15, bf16[512,128]{1,0:T(8,128)(2,1)} %bitcast.16, bf16[64,512,128]{2,1,0:T(8,128)(2,1)} %bitcast.10, ...), custom_call_target="tpu_custom_call" | custom-call | flops 9663676416 | bytes 25165824 | tf_op jit(solution)/shard_map/pallas_call | solution.py:421
  54.3 2.4 %copy.12 = bf16[64,4,16,128]{3,2,1,0:T(8,128)(2,1)} copy(bf16[64,4,16,128]{3,2,1,0:T(8,128)(2,1)} %bitcast.9) | data formatting | bytes 2097152
